TPU v7x, 256 devices: a whole 4x4x8 slice. The times are simulated.
256 devices in a mesh: row: 8 (over x, core), col: 32 (over z, y).
Axes of the slice: x: 4, y: 4, z: 8, core: 2. Of those that a mesh axis runs over, the one named last changes fastest.
Arguments:
- positions: int32 [3, 8192], P(None, ('row', 'col')), may hold values from 0 to 31, as said below
- start_vector: float32 [3, 8192, 128], P(None, ('row', 'col')), may hold values from -6 to 6
Outputs:
- displacement: float32 [3, 8192, 128], P(None, ('row', 'col'))
Inputs may be any that keep to these rules, and one draw needn't show every extreme that they name: `positions`: for each bead: x and y coordinates in 0 to 31, z coordinate in 0 to 31; no two beads share a lattice site.
All inputs are finite; a program needn't handle non-finite values.
Results may differ from a plain program's by a relative error of at most 0.0003.
Values sent between devices are 32-bit elements; how exact they have to be, the bound alone decides.
A program may use at most 64 MiB of HBM per device.

v0:
```python
import functools

import jax
import jax.numpy as jnp
from jax import lax
from jax.experimental import pallas as pl
from jax.experimental.pallas import tpu as pltpu
from jax.sharding import PartitionSpec as P

ITERS = 3
RADIUS = 0.4
MESH = pl.DeviceIdType.MESH
F32 = jnp.float32
BF16 = jnp.bfloat16

PLANE, LINE = 16, 8
PLACES = ((0, 0), (2, 0), (0, 2), (2, 2), (0, 1), (3, 0), (1, 1), (1, 3), (3, 2), (2, 1),
          (0, 3), (1, 0), (3, 3), (3, 1), (1, 2), (2, 3))
NEEDED = 10
ORDER = ((0, 1), (0, 3), (1, 0), (3, 0), (2, 0), (0, 2), (1, 1), (3, 3), (1, 3), (3, 1),
         (1, 2), (2, 1), (3, 2), (2, 3), (2, 2))
STEPS = (0, 1, 7, 2, 6, 3, 5, 4)


def seen_in_plane(dx, dy):
    return PLACES.index((-dx % 4, -dy % 4))


def seen_in_line(dz):
    return PLANE + STEPS.index(-dz % 8)


HALF = 64
BLOCK = 512
WIDTH = 768


def kernel(pos_ref, z_ref, out_ref, posrow, posbuf, colbc, lanevec, mob_high, mob_low, wide, narrow, ag, rs, rs_send,
           packed, first_dir, mate, acc, acc_wide, part, red_src, red_one, red_two, moments, flatten,
           z_mate, mate_sem, pos_sem, line_sem, plane_sem, ag_send, rs_recv, rs_sent, red_sem):
    row, col = lax.axis_index("row"), lax.axis_index("col")
    x, core = lax.div(row, 2), lax.rem(row, 2)
    z, y = lax.div(col, 4), lax.rem(col, 4)

    xs = [lax.rem(x + d, 4) for d in range(4)]
    ys = [lax.rem(y + d, 4) for d in range(4)]
    zs = [lax.rem(z + d, 8) for d in range(8)]

    def plane_at(dx, dy):
        return (xs[dx] * 2 + core, z * 4 + ys[dy])

    far_places, far_steps = PLACES[:0:-1], STEPS[:0:-1]

    def line_at(dz):
        return (row, zs[dz] * 4 + y)

    def line_mate(dz):
        return (x * 2 + 1 - core, zs[dz] * 4 + y)

    sibling = (x * 2 + 1 - core, col)

    def remote(src, dst, send, recv, device):
        return pltpu.make_async_remote_copy(
            src_ref=src, dst_ref=dst, send_sem=send, recv_sem=recv, device_id=device, device_id_type=MESH)

    def wait_recv(ref, sem):
        remote(ref, ref, sem, sem, (row, col)).wait_recv()

    def wait_send(ref, sem):
        remote(ref, ref, sem, sem, (row, col)).wait_send()

    first = lax.broadcasted_iota(jnp.int32, (32, 128), 1) < HALF
    keep = first == (core == 0)

    def turn(value):
        return pltpu.roll(value, HALF, 1)

    barrier = pltpu.get_barrier_semaphore()

    def signal(device):
        pl.semaphore_signal(barrier, inc=1, device_id=device, device_id_type=MESH)

    signal(sibling)
    for dx, dy in far_places:
        signal(plane_at(dx, dy))
    for dz in far_steps:
        signal(line_at(dz))
        signal(line_mate(dz))

    flatten[...] = jnp.zeros_like(flatten)
    flatten[0:3, 0:32] = pos_ref[...].astype(F32)
    rows3 = flatten[...]
    posrow[core] = rows3[0:1] + pltpu.roll(rows3[1:2], 32, 1) + pltpu.roll(rows3[2:3], 64, 1)
    pl.semaphore_wait(barrier, 30)

    remote(posrow.at[core], posrow.at[core], pos_sem.at[0], pos_sem.at[1], sibling).start()
    remote(z_ref, z_mate, mate_sem.at[0], mate_sem.at[1], sibling).start()
    wait_recv(posrow.at[0], pos_sem.at[1])
    both = jnp.concatenate([posrow[0], posrow[1]], axis=1)
    posbuf[0] = both
    posbuf[PLANE] = both
    for n, spot in enumerate(far_places):
        if n < 7:
            remote(posbuf.at[PLANE], posbuf.at[seen_in_line(far_steps[n])], pos_sem.at[2], pos_sem.at[3],
                   line_at(far_steps[n])).start()
        remote(posbuf.at[0], posbuf.at[seen_in_plane(*spot)], pos_sem.at[2], pos_sem.at[3], plane_at(*spot)).start()
    wait_recv(z_mate, mate_sem.at[1])
    for axis in range(3):
        packed[0, axis] = jnp.where(keep, z_ref[axis], turn(z_mate[axis]))

    def gather(step):
        def to_line():
            for dz in STEPS[1:]:
                slot = seen_in_line(dz)
                remote(packed.at[step], ag.at[step, slot], ag_send.at[step], line_sem.at[step, (slot - PLANE) // 4],
                       line_at(dz)).start()

        def to_plane(some):
            for spot in ORDER:
                slot = seen_in_plane(*spot)
                if slot < NEEDED or not some:
                    remote(packed.at[step], ag.at[step, slot], ag_send.at[step], plane_sem.at[step, slot // 8],
                           plane_at(*spot)).start()

        last = step == 2
        pl.when(core == 0)(to_line)
        pl.when(last)(lambda: to_plane(True))
        pl.when((core == 1) & jnp.logical_not(last))(lambda: to_plane(False))
        pl.when((core == 1) & last)(to_line)
        ag[step, 0] = packed[step]
        ag[step, PLANE] = packed[step]

    def wait_line(step, part_of):
        wait_recv(ag.at[step, pl.ds(0, 4 if part_of else 3)], line_sem.at[step, part_of])

    def wait_plane(step, part_of, last=False):
        if part_of == 0:
            wait_recv(ag.at[step, pl.ds(0, 7)], plane_sem.at[step, 0])
        else:
            wait_recv(ag.at[step, pl.ds(0, NEEDED - 8 if last else 8)], plane_sem.at[step, 1])

    gather(0)
    acc[...] = jnp.zeros_like(acc)
    acc_wide[...] = jnp.zeros_like(acc_wide)
    part[...] = jnp.zeros_like(part)
    ag[2, NEEDED:PLANE] = jnp.zeros((PLANE - NEEDED, 3, 32, 128), F32)
    for k in range(2):
        red_src[2 * k] = jnp.zeros((1, WIDTH), F32)
    narrow[...] = jnp.zeros_like(narrow)
    wait_recv(posbuf.at[pl.ds(0, 22)], pos_sem.at[3])

    lane_of = lax.broadcasted_iota(jnp.int32, (BLOCK, 128), 1)
    bead_of = lax.broadcasted_iota(jnp.int32, (BLOCK, 128), 0) & 31
    entry_of = lax.broadcasted_iota(jnp.int32, (128, BLOCK), 0)
    column_of = lax.broadcasted_iota(jnp.int32, (128, BLOCK), 1) & 31
    owner_of = lax.broadcasted_iota(jnp.int32, (16, BLOCK), 1) >> 5
    source_of = lax.broadcasted_iota(jnp.int32, (16, BLOCK), 0)
    ones = jnp.ones((128, 128), BF16)

    def place(at, d):
        return posbuf[at + d // 2][:, (d % 2) * 128:(d % 2) * 128 + 128]

    @pl.loop(0, 2)
    def _(h):
        rows_at = jnp.where(core == 0, h, 2) * 8
        lanes_at = jnp.where(core == 0, 2, h) * 8
        spread = jnp.concatenate([jnp.broadcast_to(place(rows_at, d), (32, 128)) for d in range(16)], axis=0)
        flat = jnp.concatenate([place(lanes_at, d) for d in range(16)], axis=0).astype(BF16)
        for axis in range(3):
            own = jnp.where(lane_of == axis * 32 + bead_of, spread, 0.0).astype(BF16)
            colbc[h, axis] = jnp.dot(own, ones, preferred_element_type=F32)
            pick = jnp.where(entry_of == axis * 32 + column_of, 1.0, 0.0).astype(BF16)
            moved = jnp.dot(flat, pick, preferred_element_type=F32)
            lanevec[h, axis:axis + 1, :] = jnp.sum(jnp.where(owner_of == source_of, moved, 0.0), axis=0, keepdims=True)

    def tile_of(t):
        return jnp.where(core == 0, lax.rem(4 - t, 4), 1 - lax.div(t, 2))

    def places(t):
        tile = tile_of(t)
        h = jnp.where(core == 0, lax.div(tile, 2), lax.rem(t, 2))
        rt = jnp.where(core == 0, lax.rem(tile, 2), tile)
        return h, jnp.where(core == 0, 0, h), pl.ds(pl.multiple_of(rt * 256, 256), 256)

    def build(t):
        h, _, span = places(t)

        @pl.loop(0, 16, unroll=2)
        def _(r):
            rows = pl.ds(pl.multiple_of(span.start + r * 16, 16), 16)
            mine = [colbc[h, axis, rows, :] for axis in range(3)]
            for tile in range(4):
                lanes = slice(tile * 128, tile * 128 + 128)
                d = [mine[axis] - lanevec[h, axis:axis + 1, lanes] for axis in range(3)]
                squared = d[0] * d[0] + d[1] * d[1] + d[2] * d[2]
                root = lax.rsqrt(jnp.where(squared > 0.5, squared, 1e30))
                inverse = root * root
                prefactor = (0.75 * RADIUS) * root
                iso = prefactor * (1.0 + (2.0 / 3.0 * RADIUS * RADIUS) * inverse)
                along = (prefactor * inverse) * (1.0 - (2.0 * RADIUS * RADIUS) * inverse)
                s = [along * d[axis] for axis in range(3)]
                parts = (s[0] * d[0] + iso, s[0] * d[1], s[0] * d[2], s[1] * d[1] + iso, s[1] * d[2],
                         s[2] * d[2] + iso)
                for k, value in enumerate(parts):
                    high = value.astype(BF16)
                    at = (tile // 2) * 1536 + k * 256 + (tile % 2) * 128
                    at = slice(at, at + 128)
                    mob_high[h, rows, at] = high
                    mob_low[h, rows, at] = (value - high.astype(F32)).astype(BF16)

    def widen(h):
        base = jnp.where(core == 0, PLANE, h * 8)

        @pl.loop(0, 8, unroll=4)
        def _(s):
            for axis in range(3):
                value = ag[0, base + s, axis]
                other = turn(value)
                for j, both in enumerate((jnp.where(first, value, other), jnp.where(first, other, value))):
                    high = both.astype(BF16).astype(F32)
                    tile = jnp.where(first, high, both - high).astype(BF16)
                    at = pl.ds(pl.multiple_of(s * 64 + j * 32, 32), 32)
                    wide[h, at, axis * 128:axis * 128 + 128] = tile
                    if axis == 0:
                        wide[h, at, 384:512] = tile

    def arrange(step, base, w, quarter, weight):
        @pl.loop(0, 4, unroll=4)
        def _(s):
            values = [ag[step, base + s, axis] * weight for axis in range(3)]
            others = [turn(value) for value in values]
            for j in range(2):
                left, right = (values, others) if j == 0 else (others, values)
                lx, ly, lz = (jnp.where(first, v, 0.0).astype(BF16) for v in left)
                ry, rz = (jnp.where(first, 0.0, v).astype(BF16) for v in right[1:])
                yx = jnp.where(first, left[1], right[0]).astype(BF16)
                for k, half, tile in ((0, 0, lx), (1, 0, yx), (2, 0, lz), (2, 1, lx), (3, 0, ry), (4, 0, rz),
                                      (4, 1, ly), (5, 1, lz)):
                    at = pl.ds(pl.multiple_of(quarter * 1536 + k * 256 + s * 64 + j * 32, 32), 32)
                    narrow[w, at, half * 128:half * 128 + 128] = tile

    def arrange_half(step, part_of):
        @pl.when(core == 0)
        def _():
            wait_line(step, part_of)
            arrange(step, PLANE + 4 * part_of, 0, part_of, 1.0)

        @pl.when(core == 1)
        def _():
            if part_of == 0:
                wait_plane(step, 0)
            else:
                pl.when(step == 1)(lambda: wait_plane(step, 1))
                pl.when(step == 2)(lambda: wait_plane(step, 1, True))

            @pl.loop(0, 2)
            def _(quarter):
                slot = 8 * part_of + 4 * quarter

                @pl.when((step == 1) | (slot < NEEDED))
                def _():
                    arrange(step, slot, part_of, quarter, jnp.where((step == 2) & (slot >= 4), 2.0, 1.0))

    def dot(left, right):
        return jnp.dot(left, right, preferred_element_type=F32)

    def product(t):
        h, w, rows = places(t)

        def both(k, lo, hi):
            total = 0.0
            for quarter in range(2):
                at = slice(quarter * 1536 + k * 256, quarter * 1536 + k * 256 + 256)
                right = wide[w, quarter * 256:quarter * 256 + 256, lo:hi]
                total = total + dot(mob_high[h, rows, at], right) + dot(mob_low[h, rows, at], right)
            return total

        xy, yz, zx = both(1, 0, 256), both(4, 128, 384), both(2, 256, 512)
        return (both(0, 0, 128) + xy[:, 128:] + zx[:, :128],
                both(3, 128, 256) + xy[:, :128] + yz[:, 128:],
                both(5, 256, 384) + zx[:, 128:] + yz[:, :128])

    def halves(i, upper):
        return pl.ds(pl.multiple_of(i * 64 + upper * 32, 32), 32)

    def pack(_, i):
        chunk = []
        for axis in range(3):
            low, high = acc[axis, halves(i, 0), :], acc[axis, halves(i, 1), :]
            chunk.append(jnp.where(first, low + turn(low), high + turn(high)))
        return chunk

    def pack_wide(tile, i):
        low, high = halves(i, 0), halves(i, 1)
        xy_low, xy_high = acc_wide[tile, low, :128], acc_wide[tile, high, :128]
        z_low, z_high = acc_wide[tile, low, 128:], acc_wide[tile, high, 128:]
        return (jnp.where(first, xy_low, turn(xy_high)), jnp.where(first, turn(xy_low), xy_high),
                jnp.where(first, z_low, turn(z_high)))

    def scatter(step, t, packer):
        def fill(tile):
            chunks = [packer(tile, i) for i in range(4)]
            for i, chunk in enumerate(chunks):
                for axis, value in enumerate(chunk):
                    rs_send[step, tile * 4 + i, axis] = value

        def send_plane(tile):
            fill(tile)
            for i in (3, 2, 1, 0):
                spot = PLACES[tile * 4 + i]
                if tile * 4 + i:
                    remote(rs_send.at[step, tile * 4 + i], rs.at[step, seen_in_plane(*spot)], rs_sent.at[step],
                           rs_recv.at[step], plane_at(*spot)).start()
                else:
                    rs[step, 0] = rs_send[step, 0]

        def send_line(tile):
            fill(tile)
            for i in (3, 2, 1, 0):
                dz = STEPS[tile * 4 + i]
                if dz:
                    remote(rs_send.at[step, tile * 4 + i], rs.at[step, seen_in_line(dz) - PLANE], rs_sent.at[step],
                           rs_recv.at[step], line_at(dz)).start()
                else:
                    rs[step, 0] = rs_send[step, 0]

        for n in range(4):
            pl.when((core == 0) & (t == n))(functools.partial(send_plane, (4 - n) % 4))
        for n in range(2):
            pl.when((core == 1) & (t == 2 * n + 1))(functools.partial(send_line, 1 - n))

    def collect(step):
        @pl.when(core == 0)
        def _():
            wait_recv(rs.at[step, pl.ds(0, PLANE - 1)], rs_recv.at[step])
            for axis in range(3):
                packed[step + 1, axis] = sum((rs[step, s, axis] for s in range(1, PLANE)), rs[step, 0, axis])

        @pl.when(core == 1)
        def _():
            wait_recv(rs.at[step, pl.ds(0, LINE - 1)], rs_recv.at[step])
            for axis in range(3):
                packed[step + 1, axis] = sum((rs[step, s, axis] for s in range(1, LINE)), rs[step, 0, axis])

    front = lax.broadcasted_iota(jnp.int32, (1, 128), 1) < HALF

    def fold(value):
        line = jnp.sum(value, axis=0, keepdims=True)
        return line + turn(line)

    def inner(left, right):
        return fold(sum(left[axis] * right[axis] for axis in range(3)))

    def reduce_plane(k, values):
        for n, value in values:
            red_src[2 * k, :, n * 128:n * 128 + 128] = value
        for spot in far_places:
            remote(red_src.at[2 * k], red_one.at[k, seen_in_plane(*spot)], red_sem.at[k, 0], red_sem.at[k, 1], plane_at(*spot)).start()
        red_one[k, 0] = red_src[2 * k]

    def reduce_line(k):
        def send(dz, device):
            slot = seen_in_line(dz) - PLANE
            remote(red_src.at[2 * k + 1], red_two.at[k, core, slot], red_sem.at[k, 2], red_sem.at[k, 3], device).start()

        wait_recv(red_one.at[k, pl.ds(0, PLANE - 1)], red_sem.at[k, 1])
        red_src[2 * k + 1] = sum((red_one[k, s] for s in range(1, PLANE)), red_one[k, 0])
        for dz in far_steps:
            send(dz, line_at(dz))
            if k == 1:
                send(dz, line_mate(dz))
        if k == 1:
            send(0, sibling)
        red_two[k, core, 0] = red_src[2 * k + 1]

    def reduced(k, c):
        return sum((red_two[k, c, s] for s in range(1, LINE)), red_two[k, c, 0])

    @pl.loop(0, 2)
    def _(t):
        build(t)

    @pl.when(core == 0)
    def _():
        wait_line(0, 0)
        wait_line(0, 1)

    @pl.when(core == 1)
    def _():
        wait_plane(0, 0)
        wait_plane(0, 1)
        widen(1)

    widen(0)

    @pl.loop(0, 4)
    def _(t):
        @pl.when(t >= 2)
        def _():
            build(t)

        more = (core == 1) & (lax.rem(t, 2) == 1)
        for axis, value in enumerate(product(t)):
            acc[axis] = jnp.where(more, acc[axis], 0.0) + value
        scatter(0, t, pack)

    collect(0)
    gather(1)
    reduce_plane(0, ((0, inner(packed.at[0], packed.at[0])), (1, inner(packed.at[0], packed.at[1]))))

    @pl.loop(1, ITERS)
    def _(step):
        def unit(part_of, t):
            tile = tile_of(t)
            quarter = jnp.where(core == 0, part_of, lax.rem(t, 2))
            h = jnp.where(core == 0, lax.div(tile, 2), part_of)
            w = jnp.where(core == 0, 0, part_of)
            rt = jnp.where(core == 0, lax.rem(tile, 2), tile)
            inner_at = pl.ds(pl.multiple_of(quarter * 1536, 1536), 1536)
            rows = pl.ds(pl.multiple_of(rt * 256, 256), 256)
            return tile, dot(mob_high[h, rows, inner_at], narrow[w, inner_at, :])

        arrange_half(step, 0)

        @pl.loop(0, 4)
        def _(t):
            @pl.when((step == 1) | (core == 1) | (t != 1))
            def _():
                tile, value = unit(0, t)
                more = (core == 1) & (lax.rem(t, 2) == 1)
                acc_wide[tile] = jnp.where(more, acc_wide[tile], 0.0) + value

        arrange_half(step, 1)

        @pl.loop(0, 4)
        def _(t):
            @pl.when((step == 1) | jnp.where(core == 1, lax.rem(t, 2) == 0, t != 1))
            def _():
                tile, value = unit(1, t)
                acc_wide[tile] += value

            @pl.when(step == 1)
            def _():
                scatter(1, t, pack_wide)

            @pl.when((step == 2) & (t == 0) & (core == 0))
            def _():
                wait_plane(2, 0)
                wait_plane(2, 1, True)

            @pl.when((step == 2) & (t == 0) & (core == 1))
            def _():
                wait_line(2, 0)
                wait_line(2, 1)

            @pl.when((step == 2) & jnp.where(core == 1, lax.rem(t, 2) == 1, t != 1))
            def _():
                tile = tile_of(t)
                at = jnp.where(core == 0, 0, PLANE) + tile * 4
                total = jnp.zeros((32, 128), F32)
                for i in range(4):
                    for axis, value in enumerate(pack_wide(tile, i)):
                        total = total + value * ag[2, at + i, axis]
                part[...] += total * jnp.where((core == 0) & (tile > 0), 2.0, 1.0)

        @pl.when(step == 1)
        def _():
            reduce_line(0)
            collect(1)
            wait_recv(red_two.at[0, 0, pl.ds(0, LINE - 1)], red_sem.at[0, 3])
            total = reduced(0, core)
            moments[0] = jnp.broadcast_to(total[:, 128:256] / total[:, 0:128], (32, 128))
            a1 = moments[0]
            for axis in range(3):
                y1 = packed[1, axis]
                packed[2, axis] = packed[2, axis] - a1 * y1
                first_dir[axis] = y1 - a1 * packed[0, axis]
            gather(2)
            remote(first_dir, mate.at[0], mate_sem.at[2], mate_sem.at[3], sibling).start()
            remote(packed.at[2], mate.at[1], mate_sem.at[2], mate_sem.at[3], sibling).start()
            early = (red_src[0][:, 0:128], red_src[0][:, 128:256], inner(first_dir, first_dir),
                     inner(first_dir, packed.at[2]), inner(packed.at[2], packed.at[2]))
            for n, value in enumerate(early):
                red_src[2, :, n * 128:n * 128 + 128] = value

    reduce_plane(1, ((5, fold(part[...])),))
    reduce_line(1)
    wait_recv(red_one.at[1, pl.ds(0, 2 * LINE - 1)], red_sem.at[1, 3])
    low, high = reduced(1, 0), reduced(1, 1)
    for k in range(6):
        at = slice(k * 128, k * 128 + 128)
        moments[k + 1, 0:8] = jnp.broadcast_to(jnp.where(front, low[:, at], high[:, at]), (8, 128))
    moments[7, 0:8] = jnp.zeros((8, 128), F32)
    moments[8, 0:8] = jnp.ones((8, 128), F32)
    m0, m1, e1, f1, g, third, zero, one = (moments[k, 0:8] for k in range(1, 9))

    a1, a2, bb2 = m1 / m0, f1 / e1, e1 / m0
    e2 = g - a2 * f1 - bb2 * e1
    bb3 = e2 / e1
    a3 = (third - a2 * g - bb2 * (f1 + a1 * e1)) / e2 - a2
    d1, d2, d3 = 1.0 + a1, 1.0 + a2, 1.0 + a3
    scale = (d1 + d2 + d3) / ITERS
    current = (d1 / scale, jnp.sqrt(bb2) / scale, zero, d2 / scale, jnp.sqrt(bb3) / scale, d3 / scale)
    partner = (one, zero, zero, one, zero, one)

    def inverse_three(m):
        c00, c01, c02 = m[3] * m[5] - m[4] * m[4], m[2] * m[4] - m[1] * m[5], m[1] * m[4] - m[2] * m[3]
        c11, c12, c22 = m[0] * m[5] - m[2] * m[2], m[1] * m[2] - m[0] * m[4], m[0] * m[3] - m[1] * m[1]
        over = 1.0 / (m[0] * c00 + m[1] * c01 + m[2] * c02)
        return tuple(c * over for c in (c00, c01, c02, c11, c12, c22))

    def newton(_, state):
        now, other = state
        return (tuple(0.5 * (u + v) for u, v in zip(now, inverse_three(other))),
                tuple(0.5 * (u + v) for u, v in zip(other, inverse_three(now))))

    current, partner = lax.fori_loop(0, 20, newton, (current, partner))
    size = jnp.sqrt(scale)
    beta = jnp.sqrt(m0)
    r1, r2, r3 = (current[k] * size for k in range(3))
    f2, f3 = beta * r2 / jnp.sqrt(e1), beta * r3 / jnp.sqrt(e2)
    wait_recv(mate, mate_sem.at[3])
    c0, c1, c2 = (jnp.concatenate([c, c, c, c], axis=0) for c in (r1 - f3 * bb2, f2 - f3 * a2, f3))
    for axis in range(3):
        out_ref[axis] = (c0 * z_ref[axis] + c1 * jnp.where(keep, first_dir[axis], turn(mate[0, axis]))
                         + c2 * jnp.where(keep, packed[2, axis], turn(mate[1, axis])))

    wait_send(posrow.at[0], pos_sem.at[0])
    wait_send(z_mate, mate_sem.at[0])
    wait_send(mate, mate_sem.at[2])
    wait_send(posbuf.at[pl.ds(0, 22)], pos_sem.at[2])
    wait_send(ag.at[2, pl.ds(0, NEEDED - 1 + LINE - 1)], ag_send.at[2])
    for k, count in enumerate((LINE - 1, 2 * LINE - 1)):
        wait_send(red_one.at[k, pl.ds(0, PLANE - 1)], red_sem.at[k, 0])
        wait_send(red_one.at[k, pl.ds(0, count)], red_sem.at[k, 2])
    for step in range(2):
        @pl.when(core == 0)
        def _(step=step):
            wait_send(ag.at[step, pl.ds(0, LINE - 1)], ag_send.at[step])
            wait_send(rs_send.at[step, pl.ds(0, PLANE - 1)], rs_sent.at[step])

        @pl.when(core == 1)
        def _(step=step):
            wait_send(ag.at[step, pl.ds(0, PLANE - 1)], ag_send.at[step])
            wait_send(rs_send.at[step, pl.ds(0, LINE - 1)], rs_sent.at[step])


def shards(positions, start_vector):
    chunk = (3, 32, 128)
    return pl.pallas_call(
        kernel,
        out_shape=jax.ShapeDtypeStruct(start_vector.shape, F32),
        in_specs=[pl.BlockSpec(memory_space=pltpu.VMEM)] * 2,
        out_specs=pl.BlockSpec(memory_space=pltpu.VMEM),
        scratch_shapes=[
            pltpu.VMEM((2, 1, 128), F32),
            pltpu.VMEM((PLANE + LINE, 1, 256), F32),
            pltpu.VMEM((2, 3, BLOCK, 128), F32),
            pltpu.VMEM((2, 8, BLOCK), F32),
            pltpu.VMEM((2, BLOCK, 6 * BLOCK), BF16),
            pltpu.VMEM((2, BLOCK, 6 * BLOCK), BF16),
            pltpu.VMEM((2, BLOCK, 512), BF16),
            pltpu.VMEM((2, 6 * BLOCK, 256), BF16),
            pltpu.VMEM((3, PLANE + LINE) + chunk, F32),
            pltpu.VMEM((2, PLANE) + chunk, F32),
            pltpu.VMEM((2, PLANE) + chunk, F32),
            pltpu.VMEM((3,) + chunk, F32),
            pltpu.VMEM(chunk, F32),
            pltpu.VMEM((2,) + chunk, F32),
            pltpu.VMEM((3, 256, 128), F32),
            pltpu.VMEM((4, 256, 256), F32),
            pltpu.VMEM((32, 128), F32),
            pltpu.VMEM((4, 1, WIDTH), F32),
            pltpu.VMEM((2, PLANE, 1, WIDTH), F32),
            pltpu.VMEM((2, 2, LINE, 1, WIDTH), F32),
            pltpu.VMEM((9, 32, 128), F32),
            pltpu.VMEM((8, 128), F32),
            pltpu.VMEM(chunk, F32),
            pltpu.SemaphoreType.DMA((4,)),
            pltpu.SemaphoreType.DMA((4,)),
            pltpu.SemaphoreType.DMA((3, 2)),
            pltpu.SemaphoreType.DMA((3, 2)),
            pltpu.SemaphoreType.DMA((3,)),
            pltpu.SemaphoreType.DMA((2,)),
            pltpu.SemaphoreType.DMA((2,)),
            pltpu.SemaphoreType.DMA((2, 4)),
        ],
        compiler_params=pltpu.CompilerParams(
            collective_id=0, has_side_effects=True, vmem_limit_bytes=40 * 1024 * 1024),
    )(positions, start_vector)


def solution(mesh):
    in_specs = (P(None, ("row", "col")), P(None, ("row", "col"), None))
    out_specs = P(None, ("row", "col"), None)
    return jax.shard_map(shards, mesh=mesh, in_specs=in_specs, out_specs=out_specs, check_vma=False)
```

profile of v0, /device:TPU:1, one launch (start us, length us, event | category | flops | bytes accessed | tf_op | source)
XLA Modules:
  0.0 75.6 jit_solution(11549041726029605662)
XLA Ops:
  0.0 0.0 copy-start
  0.0 0.8 %copy-done = f32[3,32,128]{2,1,0:T(8,128)S(1)} copy-done((f32[3,32,128]{2,1,0:T(8,128)S(1)}, f32[3,32,128]{2,1,0:T(8,128)}, u32[]{:S(2)}) %copy-start) | copy-done | bytes 49176
  0.8 0.0 copy-start.1
  0.8 0.7 copy-done.1
  1.5 73.5 %shard_map.28 = f32[3,32,128]{2,1,0:T(8,128)S(1)} custom-call(s32[3,32]{1,0:T(4,128)S(1)} %copy-done.1, f32[3,32,128]{2,1,0:T(8,128)S(1)} %copy-done), custom_call_target="tpu_custom_call" | custom-call | tf_op jit(solution)/shard_map/pallas_call | solution.py:550
  75.0 0.6 copy.4
Async XLA Ops:
  0.0 0.8 %copy-start = (f32[3,32,128]{2,1,0:T(8,128)S(1)}, f32[3,32,128]{2,1,0:T(8,128)}, u32[]{:S(2)}) copy-start(f32[3,32,128]{2,1,0:T(8,128)} %z_ref.1) | copy-start | bytes 147460
  0.8 0.7 copy-start.1
where the time goes:
time: 75.7 us; the launch traced here: 75.6 us
  Pallas kernels  73.5 us (97%)
  local copies, waits for them, and re-layouts  2.1 us (3%)
    pallas_call x1, Pallas kernels, shards(): pl.pallas_call(kernel, out_shape=jax.ShapeDtypeStruct(start_vector.shape,...  73.5 us
    unnamed x5, local copies, waits for them, and re-layouts  2.1 us

commit v1 on v0

--- a/solution.py
+++ b/solution.py
@@ -58,6 +58,11 @@
         return (x * 2 + 1 - core, zs[dz] * 4 + y)
 
     sibling = (x * 2 + 1 - core, col)
+
+    def for_each_core(program):
+        for c in range(2):
+            pl.when(core == c)(functools.partial(program, c))
+
 
     def remote(src, dst, send, recv, device):
         return pltpu.make_async_remote_copy(
@@ -108,7 +113,7 @@
     for axis in range(3):
         packed[0, axis] = jnp.where(keep, z_ref[axis], turn(z_mate[axis]))
 
-    def gather(step):
+    def gather(c, step):
         def to_line():
             for dz in STEPS[1:]:
                 slot = seen_in_line(dz)
@@ -122,11 +127,14 @@
                     remote(packed.at[step], ag.at[step, slot], ag_send.at[step], plane_sem.at[step, slot // 8],
                            plane_at(*spot)).start()
 
-        last = step == 2
-        pl.when(core == 0)(to_line)
-        pl.when(last)(lambda: to_plane(True))
-        pl.when((core == 1) & jnp.logical_not(last))(lambda: to_plane(False))
-        pl.when((core == 1) & last)(to_line)
+        if c == 0:
+            to_line()
+        if step == 2:
+            to_plane(True)
+        elif c == 1:
+            to_plane(False)
+        if c == 1 and step == 2:
+            to_line()
         ag[step, 0] = packed[step]
         ag[step, PLANE] = packed[step]
 
@@ -139,7 +147,7 @@
         else:
             wait_recv(ag.at[step, pl.ds(0, NEEDED - 8 if last else 8)], plane_sem.at[step, 1])
 
-    gather(0)
+    for_each_core(lambda c: gather(c, 0))
     acc[...] = jnp.zeros_like(acc)
     acc_wide[...] = jnp.zeros_like(acc_wide)
     part[...] = jnp.zeros_like(part)
@@ -173,21 +181,20 @@
             moved = jnp.dot(flat, pick, preferred_element_type=F32)
             lanevec[h, axis:axis + 1, :] = jnp.sum(jnp.where(owner_of == source_of, moved, 0.0), axis=0, keepdims=True)
 
-    def tile_of(t):
-        return jnp.where(core == 0, lax.rem(4 - t, 4), 1 - lax.div(t, 2))
-
-    def places(t):
-        tile = tile_of(t)
-        h = jnp.where(core == 0, lax.div(tile, 2), lax.rem(t, 2))
-        rt = jnp.where(core == 0, lax.rem(tile, 2), tile)
-        return h, jnp.where(core == 0, 0, h), pl.ds(pl.multiple_of(rt * 256, 256), 256)
-
-    def build(t):
-        h, _, span = places(t)
+    def tile_of(c, t):
+        return (4 - t) % 4 if c == 0 else 1 - t // 2
+
+    def places(c, t):
+        tile = tile_of(c, t)
+        h, rt = (tile // 2, tile % 2) if c == 0 else (t % 2, tile)
+        return h, c * h, rt * 256
+
+    def build(c, t):
+        h, _, begin = places(c, t)
 
         @pl.loop(0, 16, unroll=2)
         def _(r):
-            rows = pl.ds(pl.multiple_of(span.start + r * 16, 16), 16)
+            rows = pl.ds(pl.multiple_of(begin + r * 16, 16), 16)
             mine = [colbc[h, axis, rows, :] for axis in range(3)]
             for tile in range(4):
                 lanes = slice(tile * 128, tile * 128 + 128)
@@ -208,8 +215,8 @@
                     mob_high[h, rows, at] = high
                     mob_low[h, rows, at] = (value - high.astype(F32)).astype(BF16)
 
-    def widen(h):
-        base = jnp.where(core == 0, PLANE, h * 8)
+    def widen(c, h):
+        base = PLANE if c == 0 else h * 8
 
         @pl.loop(0, 8, unroll=4)
         def _(s):
@@ -239,33 +246,23 @@
                     at = pl.ds(pl.multiple_of(quarter * 1536 + k * 256 + s * 64 + j * 32, 32), 32)
                     narrow[w, at, half * 128:half * 128 + 128] = tile
 
-    def arrange_half(step, part_of):
-        @pl.when(core == 0)
-        def _():
+    def arrange_half(c, step, part_of):
+        if c == 0:
             wait_line(step, part_of)
             arrange(step, PLANE + 4 * part_of, 0, part_of, 1.0)
-
-        @pl.when(core == 1)
-        def _():
-            if part_of == 0:
-                wait_plane(step, 0)
-            else:
-                pl.when(step == 1)(lambda: wait_plane(step, 1))
-                pl.when(step == 2)(lambda: wait_plane(step, 1, True))
-
-            @pl.loop(0, 2)
-            def _(quarter):
+        else:
+            wait_plane(step, part_of, step == 2)
+            for quarter in range(2):
                 slot = 8 * part_of + 4 * quarter
-
-                @pl.when((step == 1) | (slot < NEEDED))
-                def _():
-                    arrange(step, slot, part_of, quarter, jnp.where((step == 2) & (slot >= 4), 2.0, 1.0))
+                if step == 1 or slot < NEEDED:
+                    arrange(step, slot, part_of, quarter, 2.0 if step == 2 and slot >= 4 else 1.0)
 
     def dot(left, right):
         return jnp.dot(left, right, preferred_element_type=F32)
 
-    def product(t):
-        h, w, rows = places(t)
+    def product(c, t):
+        h, w, begin = places(c, t)
+        rows = slice(begin, begin + 256)
 
         def both(k, lo, hi):
             total = 0.0
@@ -281,7 +278,7 @@
                 both(5, 256, 384) + zx[:, 128:] + yz[:, :128])
 
     def halves(i, upper):
-        return pl.ds(pl.multiple_of(i * 64 + upper * 32, 32), 32)
+        return slice(i * 64 + upper * 32, i * 64 + upper * 32 + 32)
 
     def pack(_, i):
         chunk = []
@@ -297,7 +294,7 @@
         return (jnp.where(first, xy_low, turn(xy_high)), jnp.where(first, turn(xy_low), xy_high),
                 jnp.where(first, z_low, turn(z_high)))
 
-    def scatter(step, t, packer):
+    def scatter(c, step, t, packer):
         def fill(tile):
             chunks = [packer(tile, i) for i in range(4)]
             for i, chunk in enumerate(chunks):
@@ -324,23 +321,13 @@
                 else:
                     rs[step, 0] = rs_send[step, 0]
 
-        for n in range(4):
-            pl.when((core == 0) & (t == n))(functools.partial(send_plane, (4 - n) % 4))
-        for n in range(2):
-            pl.when((core == 1) & (t == 2 * n + 1))(functools.partial(send_line, 1 - n))
-
-    def collect(step):
-        @pl.when(core == 0)
-        def _():
-            wait_recv(rs.at[step, pl.ds(0, PLANE - 1)], rs_recv.at[step])
-            for axis in range(3):
-                packed[step + 1, axis] = sum((rs[step, s, axis] for s in range(1, PLANE)), rs[step, 0, axis])
-
-        @pl.when(core == 1)
-        def _():
-            wait_recv(rs.at[step, pl.ds(0, LINE - 1)], rs_recv.at[step])
-            for axis in range(3):
-                packed[step + 1, axis] = sum((rs[step, s, axis] for s in range(1, LINE)), rs[step, 0, axis])
+        (send_line if c else send_plane)(tile_of(c, t))
+
+    def collect(c, step):
+        count = LINE if c else PLANE
+        wait_recv(rs.at[step, pl.ds(0, count - 1)], rs_recv.at[step])
+        for axis in range(3):
+            packed[step + 1, axis] = sum((rs[step, s, axis] for s in range(1, count)), rs[step, 0, axis])
 
     front = lax.broadcasted_iota(jnp.int32, (1, 128), 1) < HALF
 
@@ -376,112 +363,80 @@
     def reduced(k, c):
         return sum((red_two[k, c, s] for s in range(1, LINE)), red_two[k, c, 0])
 
-    @pl.loop(0, 2)
-    def _(t):
-        build(t)
-
-    @pl.when(core == 0)
-    def _():
-        wait_line(0, 0)
-        wait_line(0, 1)
-
-    @pl.when(core == 1)
-    def _():
-        wait_plane(0, 0)
-        wait_plane(0, 1)
-        widen(1)
-
-    widen(0)
-
-    @pl.loop(0, 4)
-    def _(t):
-        @pl.when(t >= 2)
-        def _():
-            build(t)
-
-        more = (core == 1) & (lax.rem(t, 2) == 1)
-        for axis, value in enumerate(product(t)):
-            acc[axis] = jnp.where(more, acc[axis], 0.0) + value
-        scatter(0, t, pack)
-
-    collect(0)
-    gather(1)
-    reduce_plane(0, ((0, inner(packed.at[0], packed.at[0])), (1, inner(packed.at[0], packed.at[1]))))
-
-    @pl.loop(1, ITERS)
-    def _(step):
-        def unit(part_of, t):
-            tile = tile_of(t)
-            quarter = jnp.where(core == 0, part_of, lax.rem(t, 2))
-            h = jnp.where(core == 0, lax.div(tile, 2), part_of)
-            w = jnp.where(core == 0, 0, part_of)
-            rt = jnp.where(core == 0, lax.rem(tile, 2), tile)
-            inner_at = pl.ds(pl.multiple_of(quarter * 1536, 1536), 1536)
-            rows = pl.ds(pl.multiple_of(rt * 256, 256), 256)
-            return tile, dot(mob_high[h, rows, inner_at], narrow[w, inner_at, :])
-
-        arrange_half(step, 0)
-
-        @pl.loop(0, 4)
-        def _(t):
-            @pl.when((step == 1) | (core == 1) | (t != 1))
-            def _():
-                tile, value = unit(0, t)
-                more = (core == 1) & (lax.rem(t, 2) == 1)
-                acc_wide[tile] = jnp.where(more, acc_wide[tile], 0.0) + value
-
-        arrange_half(step, 1)
-
-        @pl.loop(0, 4)
-        def _(t):
-            @pl.when((step == 1) | jnp.where(core == 1, lax.rem(t, 2) == 0, t != 1))
-            def _():
-                tile, value = unit(1, t)
-                acc_wide[tile] += value
-
-            @pl.when(step == 1)
-            def _():
-                scatter(1, t, pack_wide)
-
-            @pl.when((step == 2) & (t == 0) & (core == 0))
-            def _():
-                wait_plane(2, 0)
-                wait_plane(2, 1, True)
-
-            @pl.when((step == 2) & (t == 0) & (core == 1))
-            def _():
-                wait_line(2, 0)
-                wait_line(2, 1)
-
-            @pl.when((step == 2) & jnp.where(core == 1, lax.rem(t, 2) == 1, t != 1))
-            def _():
-                tile = tile_of(t)
-                at = jnp.where(core == 0, 0, PLANE) + tile * 4
-                total = jnp.zeros((32, 128), F32)
-                for i in range(4):
-                    for axis, value in enumerate(pack_wide(tile, i)):
-                        total = total + value * ag[2, at + i, axis]
-                part[...] += total * jnp.where((core == 0) & (tile > 0), 2.0, 1.0)
-
-        @pl.when(step == 1)
-        def _():
+    def steps(c):
+        for t in range(2):
+            build(c, t)
+        if c == 0:
+            wait_line(0, 0)
+            wait_line(0, 1)
+            widen(c, 0)
+        else:
+            wait_plane(0, 0)
+            wait_plane(0, 1)
+            widen(c, 0)
+            widen(c, 1)
+        for t in range(4):
+            if t >= 2:
+                build(c, t)
+            for axis, value in enumerate(product(c, t)):
+                acc[axis] = acc[axis] + value if c == 1 and t % 2 == 1 else value
+            if c == 0 or t % 2 == 1:
+                scatter(c, 0, t, pack)
+        collect(c, 0)
+        gather(c, 1)
+        reduce_plane(0, ((0, inner(packed.at[0], packed.at[0])), (1, inner(packed.at[0], packed.at[1]))))
+
+        for step in (1, 2):
+            for part_of in range(2):
+                arrange_half(c, step, part_of)
+                for t in range(4):
+                    tile = tile_of(c, t)
+                    quarter = t % 2 if c else part_of
+                    if step == 2 and (tile == 3 if c == 0 else 8 * part_of + 4 * quarter >= NEEDED):
+                        skip = True
+                    else:
+                        skip = False
+                        h, rt = (part_of, tile) if c else (tile // 2, tile % 2)
+                        inner_at = slice(quarter * 1536, quarter * 1536 + 1536)
+                        value = dot(mob_high[h, rt * 256:rt * 256 + 256, inner_at], narrow[h if c else 0, inner_at, :])
+                        begin = part_of == 0 and (c == 0 or t % 2 == 0)
+                        acc_wide[tile] = value if begin else acc_wide[tile] + value
+                    if part_of == 0 or (c == 1 and t % 2 == 0):
+                        continue
+                    if step == 1:
+                        scatter(c, 1, t, pack_wide)
+                        continue
+                    if t == c:
+                        for half in range(2):
+                            wait_line(2, half) if c else wait_plane(2, half, True)
+                    if c == 0 and skip:
+                        continue
+                    total = jnp.zeros((32, 128), F32)
+                    for i in range(4):
+                        for axis, value in enumerate(pack_wide(tile, i)):
+                            total = total + value * ag[2, (PLANE if c else 0) + tile * 4 + i, axis]
+                    part[...] += total * (2.0 if c == 0 and tile > 0 else 1.0)
+            if step == 2:
+                break
             reduce_line(0)
-            collect(1)
+            collect(c, 1)
             wait_recv(red_two.at[0, 0, pl.ds(0, LINE - 1)], red_sem.at[0, 3])
-            total = reduced(0, core)
+            total = reduced(0, c)
             moments[0] = jnp.broadcast_to(total[:, 128:256] / total[:, 0:128], (32, 128))
             a1 = moments[0]
             for axis in range(3):
                 y1 = packed[1, axis]
                 packed[2, axis] = packed[2, axis] - a1 * y1
                 first_dir[axis] = y1 - a1 * packed[0, axis]
-            gather(2)
+            gather(c, 2)
             remote(first_dir, mate.at[0], mate_sem.at[2], mate_sem.at[3], sibling).start()
             remote(packed.at[2], mate.at[1], mate_sem.at[2], mate_sem.at[3], sibling).start()
             early = (red_src[0][:, 0:128], red_src[0][:, 128:256], inner(first_dir, first_dir),
                      inner(first_dir, packed.at[2]), inner(packed.at[2], packed.at[2]))
             for n, value in enumerate(early):
                 red_src[2, :, n * 128:n * 128 + 128] = value
+
+    for_each_core(steps)
 
     reduce_plane(1, ((5, fold(part[...])),))
     reduce_line(1)

time: 75.7 us -> 75.3 us (level)
  no operation moved by 1% of the time
where the time goes in v1:
time: 75.3 us; the launch traced here: 75.1 us
  Pallas kernels  73 us (97%)
  local copies, waits for them, and re-layouts  2.1 us (3%)
    pallas_call x1, Pallas kernels, shards(): pl.pallas_call(kernel, out_shape=jax.ShapeDtypeStruct(start_vector.shape,...  73 us
    unnamed x5, local copies, waits for them, and re-layouts  2.1 us

profile of v1, /device:TPU:1, one launch (start us, length us, event | category | flops | bytes accessed | tf_op | source)
XLA Modules:
  0.0 75.1 jit_solution(12432747651462854880)
XLA Ops:
  0.0 0.0 copy-start
  0.0 0.8 %copy-done = f32[3,32,128]{2,1,0:T(8,128)S(1)} copy-done((f32[3,32,128]{2,1,0:T(8,128)S(1)}, f32[3,32,128]{2,1,0:T(8,128)}, u32[]{:S(2)}) %copy-start) | copy-done | bytes 49176
  0.8 0.0 copy-start.1
  0.8 0.7 copy-done.1
  1.5 73.0 %shard_map.28 = f32[3,32,128]{2,1,0:T(8,128)S(1)} custom-call(s32[3,32]{1,0:T(4,128)S(1)} %copy-done.1, f32[3,32,128]{2,1,0:T(8,128)S(1)} %copy-done), custom_call_target="tpu_custom_call" | custom-call | tf_op jit(solution)/shard_map/pallas_call | solution.py:505
  74.5 0.6 copy.4
Async XLA Ops:
  0.0 0.8 %copy-start = (f32[3,32,128]{2,1,0:T(8,128)S(1)}, f32[3,32,128]{2,1,0:T(8,128)}, u32[]{:S(2)}) copy-start(f32[3,32,128]{2,1,0:T(8,128)} %z_ref.1) | copy-start | bytes 147460
  0.8 0.7 copy-start.1

commit v2 on v1

--- a/solution.py
+++ b/solution.py
@@ -364,7 +364,8 @@
         return sum((red_two[k, c, s] for s in range(1, LINE)), red_two[k, c, 0])
 
     def steps(c):
-        for t in range(2):
+        built = 4 if c else 2
+        for t in range(built):
             build(c, t)
         if c == 0:
             wait_line(0, 0)
@@ -376,7 +377,7 @@
             widen(c, 0)
             widen(c, 1)
         for t in range(4):
-            if t >= 2:
+            if t >= built:
                 build(c, t)
             for axis, value in enumerate(product(c, t)):
                 acc[axis] = acc[axis] + value if c == 1 and t % 2 == 1 else value

time: 75.3 us -> 75.2 us (level)
  no operation moved by 1% of the time
where the time goes in v2:
time: 75.2 us; the launch traced here: 75 us
  Pallas kernels  72.9 us (97%)
  local copies, waits for them, and re-layouts  2.1 us (3%)
    pallas_call x1, Pallas kernels, shards(): pl.pallas_call(kernel, out_shape=jax.ShapeDtypeStruct(start_vector.shape,...  72.9 us
    unnamed x5, local copies, waits for them, and re-layouts  2.1 us

profile of v2, /device:TPU:1, one launch (start us, length us, event | category | flops | bytes accessed | tf_op | source)
XLA Modules:
  0.0 75.0 jit_solution(9654477842203509942)
XLA Ops:
  0.0 0.0 copy-start
  0.0 0.8 %copy-done = f32[3,32,128]{2,1,0:T(8,128)S(1)} copy-done((f32[3,32,128]{2,1,0:T(8,128)S(1)}, f32[3,32,128]{2,1,0:T(8,128)}, u32[]{:S(2)}) %copy-start) | copy-done | bytes 49176
  0.8 0.0 copy-start.1
  0.8 0.7 copy-done.1
  1.5 72.9 %shard_map.28 = f32[3,32,128]{2,1,0:T(8,128)S(1)} custom-call(s32[3,32]{1,0:T(4,128)S(1)} %copy-done.1, f32[3,32,128]{2,1,0:T(8,128)S(1)} %copy-done), custom_call_target="tpu_custom_call" | custom-call | tf_op jit(solution)/shard_map/pallas_call | solution.py:506
  74.4 0.6 copy.4
Async XLA Ops:
  0.0 0.8 %copy-start = (f32[3,32,128]{2,1,0:T(8,128)S(1)}, f32[3,32,128]{2,1,0:T(8,128)}, u32[]{:S(2)}) copy-start(f32[3,32,128]{2,1,0:T(8,128)} %z_ref.1) | copy-start | bytes 147460
  0.8 0.7 copy-start.1

commit v3 on v2

--- a/solution.py
+++ b/solution.py
@@ -37,7 +37,7 @@
 
 def kernel(pos_ref, z_ref, out_ref, posrow, posbuf, colbc, lanevec, mob_high, mob_low, wide, narrow, ag, rs, rs_send,
            packed, first_dir, mate, acc, acc_wide, part, red_src, red_one, red_two, moments, flatten,
-           z_mate, mate_sem, pos_sem, line_sem, plane_sem, ag_send, rs_recv, rs_sent, red_sem):
+           z_mate, halved, ag_first, first_sem, mate_sem, pos_sem, line_sem, plane_sem, ag_send, rs_recv, rs_sent, red_sem):
     row, col = lax.axis_index("row"), lax.axis_index("col")
     x, core = lax.div(row, 2), lax.rem(row, 2)
     z, y = lax.div(col, 4), lax.rem(col, 4)
@@ -54,6 +54,12 @@
     def line_at(dz):
         return (row, zs[dz] * 4 + y)
 
+    def plane_core(spot, c):
+        return (xs[spot[0]] * 2 + c, z * 4 + ys[spot[1]])
+
+    def line_core(dz, c):
+        return (x * 2 + c, zs[dz] * 4 + y)
+
     def line_mate(dz):
         return (x * 2 + 1 - core, zs[dz] * 4 + y)
 
@@ -86,8 +92,9 @@
         pl.semaphore_signal(barrier, inc=1, device_id=device, device_id_type=MESH)
 
     signal(sibling)
-    for dx, dy in far_places:
-        signal(plane_at(dx, dy))
+    for spot in far_places:
+        signal(plane_core(spot, 0))
+        signal(plane_core(spot, 1))
     for dz in far_steps:
         signal(line_at(dz))
         signal(line_mate(dz))
@@ -96,7 +103,11 @@
     flatten[0:3, 0:32] = pos_ref[...].astype(F32)
     rows3 = flatten[...]
     posrow[core] = rows3[0:1] + pltpu.roll(rows3[1:2], 32, 1) + pltpu.roll(rows3[2:3], 64, 1)
-    pl.semaphore_wait(barrier, 30)
+    for axis in range(3):
+        low, high = z_ref[axis, :16, :], z_ref[axis, 16:, :]
+        halved[0, axis] = jnp.where(first[:16], low, turn(high))
+        halved[1, axis] = jnp.where(first[:16], turn(low), high)
+    pl.semaphore_wait(barrier, 45)
 
     remote(posrow.at[core], posrow.at[core], pos_sem.at[0], pos_sem.at[1], sibling).start()
     remote(z_ref, z_mate, mate_sem.at[0], mate_sem.at[1], sibling).start()
@@ -109,9 +120,18 @@
             remote(posbuf.at[PLANE], posbuf.at[seen_in_line(far_steps[n])], pos_sem.at[2], pos_sem.at[3],
                    line_at(far_steps[n])).start()
         remote(posbuf.at[0], posbuf.at[seen_in_plane(*spot)], pos_sem.at[2], pos_sem.at[3], plane_at(*spot)).start()
-    wait_recv(z_mate, mate_sem.at[1])
-    for axis in range(3):
-        packed[0, axis] = jnp.where(keep, z_ref[axis], turn(z_mate[axis]))
+
+    for n, spot in enumerate(ORDER):
+        if n < LINE - 1:
+            dz = STEPS[n + 1]
+            remote(halved.at[0], ag_first.at[2 * seen_in_line(dz) + core], first_sem.at[0], first_sem.at[1],
+                   line_core(dz, 0)).start()
+        remote(halved.at[1], ag_first.at[2 * seen_in_plane(*spot) + core], first_sem.at[0], first_sem.at[1],
+               plane_core(spot, 1)).start()
+    own_slot = jnp.where(core == 0, 2 * PLANE, 0) + core
+    remote(halved.at[1 - core], ag_first.at[jnp.where(core == 0, 0, 2 * PLANE) + core], first_sem.at[0],
+           first_sem.at[1], sibling).start()
+    ag_first[own_slot] = halved[core]
 
     def gather(c, step):
         def to_line():
@@ -147,7 +167,6 @@
         else:
             wait_recv(ag.at[step, pl.ds(0, NEEDED - 8 if last else 8)], plane_sem.at[step, 1])
 
-    for_each_core(lambda c: gather(c, 0))
     acc[...] = jnp.zeros_like(acc)
     acc_wide[...] = jnp.zeros_like(acc_wide)
     part[...] = jnp.zeros_like(part)
@@ -216,17 +235,17 @@
                     mob_low[h, rows, at] = (value - high.astype(F32)).astype(BF16)
 
     def widen(c, h):
-        base = PLANE if c == 0 else h * 8
-
-        @pl.loop(0, 8, unroll=4)
+        base = 2 * PLANE if c == 0 else h * 16
+
+        @pl.loop(0, 16, unroll=8)
         def _(s):
             for axis in range(3):
-                value = ag[0, base + s, axis]
+                value = ag_first[base + s, axis]
                 other = turn(value)
-                for j, both in enumerate((jnp.where(first, value, other), jnp.where(first, other, value))):
+                for j, both in enumerate((jnp.where(first[:16], value, other), jnp.where(first[:16], other, value))):
                     high = both.astype(BF16).astype(F32)
-                    tile = jnp.where(first, high, both - high).astype(BF16)
-                    at = pl.ds(pl.multiple_of(s * 64 + j * 32, 32), 32)
+                    tile = jnp.where(first[:16], high, both - high).astype(BF16)
+                    at = pl.ds(pl.multiple_of(s * 32 + j * 16, 16), 16)
                     wide[h, at, axis * 128:axis * 128 + 128] = tile
                     if axis == 0:
                         wide[h, at, 384:512] = tile
@@ -367,15 +386,9 @@
         built = 4 if c else 2
         for t in range(built):
             build(c, t)
-        if c == 0:
-            wait_line(0, 0)
-            wait_line(0, 1)
-            widen(c, 0)
-        else:
-            wait_plane(0, 0)
-            wait_plane(0, 1)
-            widen(c, 0)
-            widen(c, 1)
+        wait_recv(ag_first.at[pl.ds(0, 2 * PLANE - 1 if c else 2 * LINE - 1)], first_sem.at[1])
+        for h in range(1 + c):
+            widen(c, h)
         for t in range(4):
             if t >= built:
                 build(c, t)
@@ -383,6 +396,9 @@
                 acc[axis] = acc[axis] + value if c == 1 and t % 2 == 1 else value
             if c == 0 or t % 2 == 1:
                 scatter(c, 0, t, pack)
+        wait_recv(z_mate, mate_sem.at[1])
+        for axis in range(3):
+            packed[0, axis] = jnp.where(keep, z_ref[axis], turn(z_mate[axis]))
         collect(c, 0)
         gather(c, 1)
         reduce_plane(0, ((0, inner(packed.at[0], packed.at[0])), (1, inner(packed.at[0], packed.at[1]))))
@@ -481,6 +497,7 @@
         out_ref[axis] = (c0 * z_ref[axis] + c1 * jnp.where(keep, first_dir[axis], turn(mate[0, axis]))
                          + c2 * jnp.where(keep, packed[2, axis], turn(mate[1, axis])))
 
+    wait_send(ag_first.at[pl.ds(0, PLANE + LINE - 1)], first_sem.at[0])
     wait_send(posrow.at[0], pos_sem.at[0])
     wait_send(z_mate, mate_sem.at[0])
     wait_send(mate, mate_sem.at[2])
@@ -492,12 +509,14 @@
     for step in range(2):
         @pl.when(core == 0)
         def _(step=step):
-            wait_send(ag.at[step, pl.ds(0, LINE - 1)], ag_send.at[step])
+            if step == 1:
+                wait_send(ag.at[step, pl.ds(0, LINE - 1)], ag_send.at[step])
             wait_send(rs_send.at[step, pl.ds(0, PLANE - 1)], rs_sent.at[step])
 
         @pl.when(core == 1)
         def _(step=step):
-            wait_send(ag.at[step, pl.ds(0, PLANE - 1)], ag_send.at[step])
+            if step == 1:
+                wait_send(ag.at[step, pl.ds(0, PLANE - 1)], ag_send.at[step])
             wait_send(rs_send.at[step, pl.ds(0, LINE - 1)], rs_sent.at[step])
 
 
@@ -532,6 +551,9 @@
             pltpu.VMEM((9, 32, 128), F32),
             pltpu.VMEM((8, 128), F32),
             pltpu.VMEM(chunk, F32),
+            pltpu.VMEM((2, 3, 16, 128), F32),
+            pltpu.VMEM((2 * (PLANE + LINE), 3, 16, 128), F32),
+            pltpu.SemaphoreType.DMA((2,)),
             pltpu.SemaphoreType.DMA((4,)),
             pltpu.SemaphoreType.DMA((4,)),
             pltpu.SemaphoreType.DMA((3, 2)),

time: 75.2 us -> 75.3 us (level)
  no operation moved by 1% of the time
where the time goes in v3:
time: 75.3 us; the launch traced here: 75.2 us
  Pallas kernels  73 us (97%)
  local copies, waits for them, and re-layouts  2.1 us (3%)
    pallas_call x1, Pallas kernels, shards(): pl.pallas_call(kernel, out_shape=jax.ShapeDtypeStruct(start_vector.shape,...  73 us
    unnamed x5, local copies, waits for them, and re-layouts  2.1 us

profile of v3, /device:TPU:1, one launch (start us, length us, event | category | flops | bytes accessed | tf_op | source)
XLA Modules:
  0.0 75.2 jit_solution(4533475367565323222)
XLA Ops:
  0.0 0.0 copy-start
  0.0 0.8 %copy-done = f32[3,32,128]{2,1,0:T(8,128)S(1)} copy-done((f32[3,32,128]{2,1,0:T(8,128)S(1)}, f32[3,32,128]{2,1,0:T(8,128)}, u32[]{:S(2)}) %copy-start) | copy-done | bytes 49176
  0.8 0.0 copy-start.1
  0.8 0.7 copy-done.1
  1.5 73.0 %shard_map.28 = f32[3,32,128]{2,1,0:T(8,128)S(1)} custom-call(s32[3,32]{1,0:T(4,128)S(1)} %copy-done.1, f32[3,32,128]{2,1,0:T(8,128)S(1)} %copy-done), custom_call_target="tpu_custom_call" | custom-call | tf_op jit(solution)/shard_map/pallas_call | solution.py:525
  74.5 0.6 copy.4
Async XLA Ops:
  0.0 0.8 %copy-start = (f32[3,32,128]{2,1,0:T(8,128)S(1)}, f32[3,32,128]{2,1,0:T(8,128)}, u32[]{:S(2)}) copy-start(f32[3,32,128]{2,1,0:T(8,128)} %z_ref.1) | copy-start | bytes 147460
  0.8 0.7 copy-start.1

commit v4 on v2

--- a/solution.py
+++ b/solution.py
@@ -49,7 +49,8 @@
     def plane_at(dx, dy):
         return (xs[dx] * 2 + core, z * 4 + ys[dy])
 
-    far_places, far_steps = PLACES[:0:-1], STEPS[:0:-1]
+    far_places = sorted(PLACES[1:], key=lambda spot: -min(spot[0], 4 - spot[0]) - min(spot[1], 4 - spot[1]))
+    far_steps = STEPS[:0:-1]
 
     def line_at(dz):
         return (row, zs[dz] * 4 + y)
@@ -470,7 +471,7 @@
         return (tuple(0.5 * (u + v) for u, v in zip(now, inverse_three(other))),
                 tuple(0.5 * (u + v) for u, v in zip(other, inverse_three(now))))
 
-    current, partner = lax.fori_loop(0, 20, newton, (current, partner))
+    current, partner = lax.fori_loop(0, 20, newton, (current, partner), unroll=4)
     size = jnp.sqrt(scale)
     beta = jnp.sqrt(m0)
     r1, r2, r3 = (current[k] * size for k in range(3))

time: 75.2 us -> 75.2 us (level)
  no operation moved by 1% of the time
where the time goes in v4:
time: 75.2 us; the launch traced here: 75 us
  Pallas kernels  72.9 us (97%)
  local copies, waits for them, and re-layouts  2.1 us (3%)
    pallas_call x1, Pallas kernels, shards(): pl.pallas_call(kernel, out_shape=jax.ShapeDtypeStruct(start_vector.shape,...  72.9 us
    unnamed x5, local copies, waits for them, and re-layouts  2.1 us

profile of v4, /device:TPU:1, one launch (start us, length us, event | category | flops | bytes accessed | tf_op | source)
XLA Modules:
  0.0 75.0 jit_solution(12118885885075447417)
XLA Ops:
  0.0 0.0 copy-start
  0.0 0.8 %copy-done = f32[3,32,128]{2,1,0:T(8,128)S(1)} copy-done((f32[3,32,128]{2,1,0:T(8,128)S(1)}, f32[3,32,128]{2,1,0:T(8,128)}, u32[]{:S(2)}) %copy-start) | copy-done | bytes 49176
  0.8 0.0 copy-start.1
  0.8 0.7 copy-done.1
  1.5 72.9 %shard_map.28 = f32[3,32,128]{2,1,0:T(8,128)S(1)} custom-call(s32[3,32]{1,0:T(4,128)S(1)} %copy-done.1, f32[3,32,128]{2,1,0:T(8,128)S(1)} %copy-done), custom_call_target="tpu_custom_call" | custom-call | tf_op jit(solution)/shard_map/pallas_call | solution.py:507
  74.4 0.6 copy.4
Async XLA Ops:
  0.0 0.8 %copy-start = (f32[3,32,128]{2,1,0:T(8,128)S(1)}, f32[3,32,128]{2,1,0:T(8,128)}, u32[]{:S(2)}) copy-start(f32[3,32,128]{2,1,0:T(8,128)} %z_ref.1) | copy-start | bytes 147460
  0.8 0.7 copy-start.1

commit v5 on v2

--- a/solution.py
+++ b/solution.py
@@ -392,17 +392,17 @@
                 arrange_half(c, step, part_of)
                 for t in range(4):
                     tile = tile_of(c, t)
-                    quarter = t % 2 if c else part_of
-                    if step == 2 and (tile == 3 if c == 0 else 8 * part_of + 4 * quarter >= NEEDED):
-                        skip = True
-                    else:
-                        skip = False
-                        h, rt = (part_of, tile) if c else (tile // 2, tile % 2)
-                        inner_at = slice(quarter * 1536, quarter * 1536 + 1536)
-                        value = dot(mob_high[h, rt * 256:rt * 256 + 256, inner_at], narrow[h if c else 0, inner_at, :])
-                        begin = part_of == 0 and (c == 0 or t % 2 == 0)
-                        acc_wide[tile] = value if begin else acc_wide[tile] + value
-                    if part_of == 0 or (c == 1 and t % 2 == 0):
+                    if c == 1 and t % 2 == 0:
+                        continue
+                    skip = c == 0 and step == 2 and tile == 3
+                    if not skip:
+                        if c == 0:
+                            h, rt, w, inner_at = tile // 2, tile % 2, 0, slice(part_of * 1536, part_of * 1536 + 1536)
+                        else:
+                            h, rt, w, inner_at = part_of, tile, part_of, slice(0, 1536 * (2 - part_of * (step - 1)))
+                        value = dot(mob_high[h, rt * 256:rt * 256 + 256, inner_at], narrow[w, inner_at, :])
+                        acc_wide[tile] = acc_wide[tile] + value if part_of else value
+                    if part_of == 0:
                         continue
                     if step == 1:
                         scatter(c, 1, t, pack_wide)

time: 75.2 us -> 75.2 us (level)
  no operation moved by 1% of the time
where the time goes in v5:
time: 75.2 us; the launch traced here: 75 us
  Pallas kernels  72.9 us (97%)
  local copies, waits for them, and re-layouts  2.1 us (3%)
    pallas_call x1, Pallas kernels, shards(): pl.pallas_call(kernel, out_shape=jax.ShapeDtypeStruct(start_vector.shape,...  72.9 us
    unnamed x5, local copies, waits for them, and re-layouts  2.1 us

profile of v5, /device:TPU:1, one launch (start us, length us, event | category | flops | bytes accessed | tf_op | source)
XLA Modules:
  0.0 75.0 jit_solution(9654477842203509942)
XLA Ops:
  0.0 0.0 copy-start
  0.0 0.8 %copy-done = f32[3,32,128]{2,1,0:T(8,128)S(1)} copy-done((f32[3,32,128]{2,1,0:T(8,128)S(1)}, f32[3,32,128]{2,1,0:T(8,128)}, u32[]{:S(2)}) %copy-start) | copy-done | bytes 49176
  0.8 0.0 copy-start.1
  0.8 0.7 copy-done.1
  1.5 72.9 %shard_map.28 = f32[3,32,128]{2,1,0:T(8,128)S(1)} custom-call(s32[3,32]{1,0:T(4,128)S(1)} %copy-done.1, f32[3,32,128]{2,1,0:T(8,128)S(1)} %copy-done), custom_call_target="tpu_custom_call" | custom-call | tf_op jit(solution)/shard_map/pallas_call | solution.py:506
  74.4 0.6 copy.4
Async XLA Ops:
  0.0 0.8 %copy-start = (f32[3,32,128]{2,1,0:T(8,128)S(1)}, f32[3,32,128]{2,1,0:T(8,128)}, u32[]{:S(2)}) copy-start(f32[3,32,128]{2,1,0:T(8,128)} %z_ref.1) | copy-start | bytes 147460
  0.8 0.7 copy-start.1

commit v6 on v5

--- a/solution.py
+++ b/solution.py
@@ -121,7 +121,7 @@
                        line_at(dz)).start()
 
         def to_plane(some):
-            for spot in ORDER:
+            for spot in sorted(ORDER, key=lambda spot: seen_in_plane(*spot) // 8):
                 slot = seen_in_plane(*spot)
                 if slot < NEEDED or not some:
                     remote(packed.at[step], ag.at[step, slot], ag_send.at[step], plane_sem.at[step, slot // 8],

time: 75.2 us -> 74 us (0.984)
  Pallas kernels: 72.9 us -> 71.7 us
    pallas_call x1, Pallas kernels: 72.9 us -> 71.7 us  [shards(): pl.pallas_call(kernel, out_shape=jax.ShapeDtypeStruct(start_vector.shape,...]
where the time goes in v6:
time: 74 us; the launch traced here: 73.8 us
  Pallas kernels  71.7 us (97%)
  local copies, waits for them, and re-layouts  2.1 us (3%)
    pallas_call x1, Pallas kernels, shards(): pl.pallas_call(kernel, out_shape=jax.ShapeDtypeStruct(start_vector.shape,...  71.7 us
    unnamed x5, local copies, waits for them, and re-layouts  2.1 us

profile of v6, /device:TPU:1, one launch (start us, length us, event | category | flops | bytes accessed | tf_op | source)
XLA Modules:
  0.0 73.8 jit_solution(648659108516547226)
XLA Ops:
  0.0 0.0 copy-start
  0.0 0.8 %copy-done = f32[3,32,128]{2,1,0:T(8,128)S(1)} copy-done((f32[3,32,128]{2,1,0:T(8,128)S(1)}, f32[3,32,128]{2,1,0:T(8,128)}, u32[]{:S(2)}) %copy-start) | copy-done | bytes 49176
  0.8 0.0 copy-start.1
  0.8 0.7 copy-done.1
  1.5 71.7 %shard_map.28 = f32[3,32,128]{2,1,0:T(8,128)S(1)} custom-call(s32[3,32]{1,0:T(4,128)S(1)} %copy-done.1, f32[3,32,128]{2,1,0:T(8,128)S(1)} %copy-done), custom_call_target="tpu_custom_call" | custom-call | tf_op jit(solution)/shard_map/pallas_call | solution.py:506
  73.2 0.6 copy.4
Async XLA Ops:
  0.0 0.8 %copy-start = (f32[3,32,128]{2,1,0:T(8,128)S(1)}, f32[3,32,128]{2,1,0:T(8,128)}, u32[]{:S(2)}) copy-start(f32[3,32,128]{2,1,0:T(8,128)} %z_ref.1) | copy-start | bytes 147460
  0.8 0.7 copy-start.1
